TPU v7x, 512 devices: a whole 4x4x16 slice. The times are simulated.
512 devices in a mesh: img: 64 (over y, z_lo, x), tpl: 4 (over z_hi), pix: 2 (over core).
Axes of the slice: x: 4, y: 4, z: 16 (z_hi: 4, z_lo: 4; z = z_hi * 4 + z_lo), core: 2. Of those that a mesh axis runs over, the one named last changes fastest.
Arguments:
- images: bfloat16 [16384, 128, 128], P(('img', 'tpl'), 'pix'), may hold values from -6 to 6
- conformers: float32 [8, 3, 4096], replicated, may hold values from -96 to 96
- atom_types: int32 [4096], replicated, may hold values from 0 to 4
- type_amp: float32 [5], replicated, may hold values from 0.3 to 3
- type_width: float32 [5], replicated, may hold values from 0.8 to 2.5
- view_angles: float32 [256, 3], replicated, may hold values from -3.140625 to 3.140625
- template_conf: int32 [512], P(('tpl', 'img')), may hold values from 0 to 7
- template_view: int32 [512], P(('tpl', 'img')), may hold values from 0 to 255
- group_ids: int32 [16384], P('img'), may hold values from 0 to 255
- group_prec: float32 [256], replicated, may hold values from 0.3 to 45
Outputs:
- averages: float32 [512, 128, 128], P(('tpl', 'img'), 'pix')
- loglik: float32 [16384], P(('img', 'tpl'))
All inputs are finite; a program needn't handle non-finite values.
Results may differ from a plain program's by a relative error of at most 0.013.
Values may be sent and summed in bfloat16 or wider, within the bound.
A program may use at most 64 MiB of HBM per device.

v0:
```python
import jax
import jax.numpy as jnp
from jax import lax
from jax.sharding import PartitionSpec as P


def atom_tables(atom_types, type_amp, type_width):
    hits = atom_types[:, None] == jnp.arange(type_amp.shape[0], dtype=jnp.int32)[None, :]
    atom_amp = jnp.sum(jnp.where(hits, type_amp[None, :], 0.0), axis=1) * 0.0625
    widths = jnp.sum(jnp.where(hits, type_width[None, :], 0.0), axis=1)
    return (atom_amp, 0.5 / (widths * widths))


def view_rows(angles):
    cos_phi = jnp.cos(angles[0])
    sin_phi = jnp.sin(angles[0])
    cos_theta = jnp.cos(angles[1])
    sin_theta = jnp.sin(angles[1])
    cos_psi = jnp.cos(angles[2])
    sin_psi = jnp.sin(angles[2])
    first_row = (
        cos_phi * cos_theta * cos_psi - sin_phi * sin_psi,
        -cos_phi * cos_theta * sin_psi - sin_phi * cos_psi,
        cos_phi * sin_theta,
    )
    second_row = (
        sin_phi * cos_theta * cos_psi + cos_phi * sin_psi,
        -sin_phi * cos_theta * sin_psi + cos_phi * cos_psi,
        sin_phi * sin_theta,
    )
    return (first_row, second_row)


def render_one(coords, angles, atom_amp, inv_spread, row_pos, col_pos):
    first_row, second_row = view_rows(angles)
    across = first_row[0] * coords[0] + first_row[1] * coords[1] + first_row[2] * coords[2]
    down = second_row[0] * coords[0] + second_row[1] * coords[1] + second_row[2] * coords[2]
    col_table = jnp.exp(-jnp.square(col_pos[None, :] - across[:, None]) * inv_spread[:, None])
    row_table = atom_amp[:, None] * jnp.exp(
        -jnp.square(row_pos[None, :] - down[:, None]) * inv_spread[:, None]
    )
    return lax.dot_general(
        row_table,
        col_table,
        (((0,), (0,)), ((), ())),
        precision=lax.Precision.HIGHEST,
        preferred_element_type=jnp.float32,
    )


def group_lookup(group_ids, group_prec):
    hits = group_ids[:, None] == jnp.arange(group_prec.shape[0], dtype=jnp.int32)[None, :]
    return jnp.sum(jnp.where(hits, group_prec[None, :], 0.0), axis=1)


def on_device(
    images,
    conformers,
    atom_types,
    type_amp,
    type_width,
    view_angles,
    template_conf,
    template_view,
    group_ids,
    group_prec,
):
    img_dev, half_rows, side = images.shape
    pixel_count = half_rows * side
    flat_rows = images.reshape(img_dev, pixel_count)
    pix_index = lax.axis_index("pix")
    tpl_index = lax.axis_index("tpl")
    tpl_count = lax.axis_size("tpl")
    atom_amp, inv_spread = atom_tables(atom_types, type_amp, type_width)
    col_pos = jnp.arange(side).astype(jnp.float32) - side * 0.5 + 0.5
    row_pos = (
        (pix_index * half_rows + jnp.arange(half_rows, dtype=jnp.int32)).astype(jnp.float32)
        - side * 0.5
        + 0.5
    )
    own_coords = jnp.take(conformers, template_conf, axis=0)
    own_angles = jnp.take(view_angles, template_view, axis=0)
    own_rendered = jax.vmap(
        lambda coords, angles: render_one(coords, angles, atom_amp, inv_spread, row_pos, col_pos)
    )(own_coords, own_angles)
    rendered_count = own_rendered.shape[0]
    own_rendered = own_rendered.astype(jnp.bfloat16).reshape(rendered_count, pixel_count)
    templates = lax.all_gather(own_rendered, "img", axis=0, tiled=True)
    tpl_dev = templates.shape[0]
    part_norms = jnp.sum(jnp.square(templates.astype(jnp.float32)), axis=1)
    precision_rows = group_lookup(group_ids, group_prec)
    img_grp = precision_rows.shape[0]
    group_images = lax.all_gather(flat_rows, "tpl", axis=0, tiled=True)
    part_scores = lax.dot_general(
        group_images, templates, (((1,), (1,)), ((), ())), preferred_element_type=jnp.float32
    )
    anchor = jnp.zeros((), jnp.int32)
    score_block = lax.dynamic_update_slice(
        jnp.zeros((img_grp, tpl_dev * tpl_count), jnp.float32),
        part_scores,
        (anchor, tpl_index * tpl_dev),
    )
    norm_block = lax.dynamic_update_slice(
        jnp.zeros((tpl_dev * tpl_count,), jnp.float32), part_norms, (tpl_index * tpl_dev,)
    )
    full_scores, full_norms = lax.psum((score_block, norm_block), ("tpl", "pix"))
    logits = precision_rows[:, None] * full_scores * lax.rsqrt(full_norms + 1e-06)[None, :]
    maximum = jnp.max(logits, axis=1)
    weights = jnp.exp(logits - maximum[:, None])
    totals = jnp.sum(weights, axis=1)
    own_weights = lax.dynamic_slice_in_dim(weights, tpl_index * tpl_dev, tpl_dev, 1)
    resp = (own_weights / totals[:, None]).astype(jnp.bfloat16)
    loglik = maximum + jnp.log(totals)
    own_loglik = lax.dynamic_slice_in_dim(loglik, tpl_index * img_dev, img_dev, 0)
    own_sums = lax.psum_scatter(
        lax.dot_general(
            resp, group_images, (((0,), (0,)), ((), ())), preferred_element_type=jnp.float32
        ),
        "img",
        scatter_dimension=0,
        tiled=True,
    )
    part_squares = jnp.sum(jnp.square(own_sums), axis=1)
    full_squares = lax.psum(part_squares, "pix")
    scale = lax.rsqrt(full_squares / (side * side) + 1e-06)
    averages = (own_sums * scale[:, None]).reshape(rendered_count, half_rows, side)
    return (averages, own_loglik)


def solution(mesh):
    placed = (
        P(("img", "tpl"), "pix", None),
        P(),
        P(),
        P(),
        P(),
        P(),
        P(("tpl", "img")),
        P(("tpl", "img")),
        P("img"),
        P(),
    )
    return jax.shard_map(
        on_device,
        mesh=mesh,
        in_specs=placed,
        out_specs=(P(("tpl", "img"), "pix", None), P(("img", "tpl"))),
        check_vma=False,
    )
```

profile of v0, /device:TPU:1, one launch (start us, length us, event | category | flops | bytes accessed | tf_op | source)
XLA Modules:
  0.0 1392.9 jit_solution(15018643670695546310)
XLA Ops:
  7.2 0.7 compare_select_fusion
  7.9 0.7 compare_and_fusion
  8.6 0.8 copy.15
  9.5 0.6 gather_fusion
  10.1 0.3 add_reduce_fusion.1
  10.4 0.9 gather_fusion.1
  11.4 0.1 broadcast_select_fusion
  11.5 0.9 select_reduce_fusion.2
  12.4 0.1 multiply_add_fusion.1
  12.5 4.2 fusion.16
  16.7 0.6 reshape.202
  17.4 1.7 copy.20
  19.2 314.0 %all-gather.6.cloned.1.call-done = bf16[64,2,8192]{2,1,0:T(2,128)(2,1)} async-done(((bf16[1,2,8192]{2,1,0:T(2,128)(2,1)}), bf16[64,2,8192]{2,1,0:T(2,128)(2,1)}) %all-gather.6.cloned.1.call-update) | async-done | bytes 2097168 | tf_op jit(solution)/shard_map/all_gather | solution.py:88
  333.2 2.7 reshape.203
  336.0 204.9 %all-gather.4.cloned.1.call-done = bf16[256,8192]{1,0:T(8,128)(2,1)} async-done(((bf16[64,8192]{1,0:T(8,128)(2,1)}), bf16[256,8192]{1,0:T(8,128)(2,1)}) %all-gather.4.cloned.1.call-update) | async-done | bytes 4194320 | tf_op jit(solution)/shard_map/all_gather | solution.py:93
  540.9 3.7 fusion.15
  544.7 0.8 copy-done.1
  545.6 0.2 select_reduce_fusion
  545.7 0.5 multiply_reduce_fusion
  546.2 0.2 dynamic_update_slice.7
  546.5 18.4 %psum.22 = f32[512]{0:T(512)S(1)} all-reduce(f32[512]{0:T(512)S(1)} %dynamic_update_slice.7), channel_id=1, replica_groups=mesh['img'=64,'tpl'=4,'pix'=2] {'tpl','pix'}, use_global_device_ids=true, to_apply=%region_5.6 | all-reduce | flops 512 | bytes 4096 | tf_op jit(solution)/shard_map/psum | solution.py:106
  564.8 77.6 %all-reduce.4.cloned.1.call-done = f32[256,512]{0,1:T(8,128)} async-done(((f32[256,512]{0,1:T(8,128)}), f32[256,512]{0,1:T(8,128)}) %all-reduce.4.cloned.1.call-update) | async-done | bytes 524304 | tf_op jit(solution)/shard_map/psum | solution.py:106
  642.5 1.2 fusion.25
  643.6 1.2 fusion.29
  644.9 4.9 fusion.26
  649.8 1.3 dynamic-slice
  651.7 683.5 %all-reduce.6.cloned.1.call-done = f32[128,8192]{1,0:T(8,128)} async-done(((f32[128,8192]{1,0:T(8,128)}), f32[128,8192]{1,0:T(8,128)}) %all-reduce.6.cloned.1.call-update) | async-done | bytes 4194320
  1335.2 1.1 multiply_reduce_fusion.1
  1336.4 0.6 dynamic_slice.7
  1336.9 47.7 %psum.23 = f32[2]{0:T(128)S(1)} all-reduce(f32[2]{0:T(128)S(1)} %multiply_reduce_fusion.1), channel_id=1, replica_groups=mesh['img'=64,'tpl'=4,'pix'=2] {'pix'}, use_global_device_ids=true, to_apply=%region_10.11 | all-reduce | flops 2 | bytes 16 | tf_op jit(solution)/shard_map/psum | solution.py:124
  1384.7 1.0 multiply_bitcast_fusion
  1385.7 0.6 copy.21
  (28 shorter events, 0.4 us)
Async XLA Ops:
  7.2 3.3 copy-start
  7.2 326.1 %all-gather.6.cloned.1.call-start = ((), (), s32[]{:S(2)}) async-start(), calls=%async_computation.2 | async-start | bytes 2129920 | tf_op jit(solution)/shard_map/all_gather | solution.py:88
  12.5 4.9 copy-start.2
  17.4 523.5 %all-gather.4.cloned.1.call-start = ((), (), s32[]{:S(2)}) async-start(), calls=%async_computation | async-start | bytes 5242880 | tf_op jit(solution)/shard_map/all_gather | solution.py:93
  19.2 623.3 %all-reduce.4.cloned.1.call-start = ((), (), s32[]{:S(2)}) async-start(), calls=%async_computation.1 | async-start | bytes 1048576 | tf_op jit(solution)/shard_map/psum | solution.py:106
  336.0 209.6 %copy-start.3 = (f32[256]{0:T(256)S(1)}, f32[256]{0:T(256)}, u32[]{:S(2)}) copy-start(f32[256]{0:T(256)} %param.19) | copy-start | bytes 3076
  336.0 209.6 %copy-start.4 = (s32[256]{0:T(256)S(1)}, s32[256]{0:T(256)}, u32[]{:S(2)}) copy-start(s32[256]{0:T(256)} %param.18) | copy-start | bytes 3076
  544.6 0.8 copy-start.1
  545.5 789.7 %all-reduce.6.cloned.1.call-start = ((), (), s32[]{:S(2)}) async-start(), calls=%async_computation.3 | async-start | bytes 8388608
Sparse Core Ops, SparseCore 0:
  17.5 315.6 all-gather.5
  335.3 205.4 all-gather.3
  545.6 96.7 all-reduce.3
  649.9 685.2 all-reduce.5
where the time goes:
time: 1390 us
  waiting for transfers between devices  1280 us (92%)
  blocking collectives  66.1 us (5%)
  between operations  14.6 us (1%)
    unnamed x5, waiting for transfers between devices  684 us
    all_gather x1, waiting for transfers between devices, on_device(): templates = lax.all_gather(own_rendered, 'img', axis=0, tiled=True)  314 us
    all_gather x1, waiting for transfers between devices, on_device(): group_images = lax.all_gather(flat_rows, 'tpl', axis=0, tiled=True)  205 us
    psum x1, waiting for transfers between devices, on_device(): lax.psum((score_block, norm_block), ('tpl', 'pix'))  77.6 us
    psum x1, blocking collectives, on_device(): full_squares = lax.psum(part_squares, 'pix')  47.7 us
  transfers between devices with their start and end apart: 4, of which 4 were waited for; matrix products, arithmetic and copies ran while one was open for 0% of the time, Pallas kernels for 0%

commit v1 on v0

--- a/solution.py
+++ b/solution.py
@@ -85,7 +85,10 @@
     )(own_coords, own_angles)
     rendered_count = own_rendered.shape[0]
     own_rendered = own_rendered.astype(jnp.bfloat16).reshape(rendered_count, pixel_count)
-    templates = lax.all_gather(own_rendered, "img", axis=0, tiled=True)
+    count = lax.axis_size("img")
+    tiles = jnp.stack([own_rendered for _ in range(count)])
+    tiles = lax.all_to_all(tiles, "img", split_axis=0, concat_axis=0)
+    templates = jnp.concatenate(tiles, axis=0)
     tpl_dev = templates.shape[0]
     part_norms = jnp.sum(jnp.square(templates.astype(jnp.float32)), axis=1)
     precision_rows = group_lookup(group_ids, group_prec)

time: 1390 us -> 1070 us (0.77)
  waiting for transfers between devices: 1280 us -> 927 us
  blocking collectives: 66.1 us -> 82.6 us
    all_gather x1 -> x0, waiting for transfers between devices: 314 us -> none  [on_device(): templates = lax.all_gather(own_rendered, 'img', axis=0, tiled=True)]
    all_gather x1, waiting for transfers between devices: 205 us -> 0.01 us  [on_device(): group_images = lax.all_gather(flat_rows, 'tpl', axis=0, tiled=True)]
    all_to_all x0 -> x1, waiting for transfers between devices: none -> 141 us  [on_device(): tiles = lax.all_to_all(tiles, 'img', split_axis=0, concat_axis=0)]
    psum x1, waiting for transfers between devices: 77.6 us -> 102 us  [on_device(): lax.psum((score_block, norm_block), ('tpl', 'pix'))]
    psum x1, blocking collectives: 18.4 us -> 34.9 us  [on_device(): lax.psum((score_block, norm_block), ('tpl', 'pix'))]
    unnamed x5 -> x4, waiting for transfers between devices: 684 us -> 684 us
  transfers between devices with their start and end apart: 4 -> 4, of which waited for: 4 -> 3; matrix products, arithmetic and copies ran while one was open for 0% -> 1% of each run, Pallas kernels for 0% -> 0%
where the time goes in v1:
time: 1070 us
  waiting for transfers between devices  927 us (87%)
  blocking collectives  82.6 us (8%)
  between operations  14.6 us (1%)
  local copies, waits for them, and re-layouts  13.5 us (1%)
  matrix products  13.5 us (1%)
  starting transfers between devices  12.9 us (1%)
    unnamed x4, waiting for transfers between devices  684 us
    all_to_all x1, waiting for transfers between devices, on_device(): tiles = lax.all_to_all(tiles, 'img', split_axis=0, concat_axis=0)  141 us
    psum x1, waiting for transfers between devices, on_device(): lax.psum((score_block, norm_block), ('tpl', 'pix'))  102 us
    psum x1, blocking collectives, on_device(): full_squares = lax.psum(part_squares, 'pix')  47.7 us
    psum x1, blocking collectives, on_device(): lax.psum((score_block, norm_block), ('tpl', 'pix'))  34.9 us
  transfers between devices with their start and end apart: 4, of which 3 were waited for; matrix products, arithmetic and copies ran while one was open for 1% of the time, Pallas kernels for 0%

profile of v1, /device:TPU:1, one launch (start us, length us, event | category | flops | bytes accessed | tf_op | source)
XLA Modules:
  0.0 1073.7 jit_solution(3991209022586128116)
XLA Ops:
  7.2 0.7 compare_and_fusion
  7.9 0.7 compare_select_fusion
  8.6 0.8 copy.23
  9.4 0.6 gather_fusion
  10.1 0.3 add_reduce_fusion.1
  10.4 0.9 select_reduce_fusion.2
  11.3 0.9 gather_fusion.1
  12.5 4.2 fusion.21
  16.7 3.4 stack.3
  20.1 12.5 %all-to-all-start = ((bf16[64,2,8192]{2,1,0:T(2,128)(2,1)}), bf16[64,2,8192]{2,1,0:T(2,128)(2,1)S(1)}, u32[]{:S(2)}, u32[]{:S(2)}) async-start(bf16[64,2,8192]{2,1,0:T(2,128)(2,1)} %stack.3), calls=%async_computation | async-start | bytes 4194304 | tf_op jit(solution)/shard_map/all_to_all | solution.py:90
  32.7 1.7 copy.33
  34.5 141.3 %all-to-all-done = bf16[64,2,8192]{2,1,0:T(2,128)(2,1)S(1)} async-done(((bf16[64,2,8192]{2,1,0:T(2,128)(2,1)}), bf16[64,2,8192]{2,1,0:T(2,128)(2,1)S(1)}, u32[]{:S(2)}, u32[]{:S(2)}) %all-to-all-start) | async-done | bytes 2097184 | tf_op jit(solution)/shard_map/all_to_all | solution.py:90
  175.8 2.2 reshape.184
  178.1 4.4 fusion.15
  182.5 0.8 copy-done.1
  183.3 0.2 all-reduce.6.cloned.1.call-start
  183.6 0.2 select_reduce_fusion
  183.8 2.3 multiply_reduce_fusion
  186.1 0.1 reduce_sum.60
  186.3 0.2 dynamic_update_slice.7
  186.5 34.9 %psum.22 = f32[512]{0:T(512)S(1)} all-reduce(f32[512]{0:T(512)S(1)} %dynamic_update_slice.7), channel_id=1, replica_groups=mesh['img'=64,'tpl'=4,'pix'=2] {'tpl','pix'}, use_global_device_ids=true, to_apply=%region_5.6 | all-reduce | flops 512 | bytes 4096 | tf_op jit(solution)/shard_map/psum | solution.py:109
  221.4 101.6 %all-reduce.4.cloned.1.call-done = f32[256,512]{0,1:T(8,128)} async-done(((f32[256,512]{0,1:T(8,128)}), f32[256,512]{0,1:T(8,128)}) %all-reduce.4.cloned.1.call-update) | async-done | bytes 524304 | tf_op jit(solution)/shard_map/psum | solution.py:109
  323.1 1.2 fusion.30
  324.3 1.2 fusion.34
  325.5 4.9 fusion.31
  330.4 1.3 dynamic-slice
  332.3 683.8 %all-reduce.6.cloned.1.call-done = f32[128,8192]{1,0:T(8,128)} async-done(((f32[128,8192]{1,0:T(8,128)}), f32[128,8192]{1,0:T(8,128)}) %all-reduce.6.cloned.1.call-update) | async-done | bytes 4194320
  1016.1 1.1 multiply_reduce_fusion.1
  1017.2 0.6 dynamic_slice.7
  1017.8 47.7 %psum.23 = f32[2]{0:T(128)S(1)} all-reduce(f32[2]{0:T(128)S(1)} %multiply_reduce_fusion.1), channel_id=1, replica_groups=mesh['img'=64,'tpl'=4,'pix'=2] {'pix'}, use_global_device_ids=true, to_apply=%region_10.11 | all-reduce | flops 2 | bytes 16 | tf_op jit(solution)/shard_map/psum | solution.py:127
  1065.5 1.0 multiply_bitcast_fusion
  1066.6 0.6 copy.34
  (30 shorter events, 0.7 us)
Async XLA Ops:
  7.2 4.1 copy-start
  16.7 16.0 %copy-start.2 = (bf16[64,64,128]{2,1,0:T(8,128)(2,1)S(1)}, bf16[64,64,128]{2,1,0:T(8,128)(2,1)}, u32[]{:S(2)}) copy-start(bf16[64,64,128]{2,1,0:T(8,128)(2,1)} %param.10) | copy-start | bytes 3145732
  20.1 155.8 %all-to-all-start = ((bf16[64,2,8192]{2,1,0:T(2,128)(2,1)}), bf16[64,2,8192]{2,1,0:T(2,128)(2,1)S(1)}, u32[]{:S(2)}, u32[]{:S(2)}) async-start(bf16[64,2,8192]{2,1,0:T(2,128)(2,1)} %stack.3), calls=%async_computation | async-start | bytes 4194304 | tf_op jit(solution)/shard_map/all_to_all | solution.py:90
  32.6 145.4 %all-gather.2.cloned.1.call-start = ((), (), s32[]{:S(2)}) async-start(), calls=%async_computation.1 | async-start | bytes 5242880 | tf_op jit(solution)/shard_map/all_gather | solution.py:96
  34.4 288.6 %all-reduce.4.cloned.1.call-start = ((), (), s32[]{:S(2)}) async-start(), calls=%async_computation.2 | async-start | bytes 1048576 | tf_op jit(solution)/shard_map/psum | solution.py:109
  178.1 5.5 copy-start.3
  178.1 5.5 copy-start.4
  182.5 0.8 copy-start.1
  183.3 832.8 %all-reduce.6.cloned.1.call-start = ((), (), s32[]{:S(2)}) async-start(), calls=%async_computation.3 | async-start | bytes 8388608
Sparse Core Ops, SparseCore 0:
  35.6 127.9 all-gather.1
  183.4 139.5 all-reduce.3
  330.5 685.5 all-reduce.5
